TPU v7x, 32 devices: a whole 2x2x4 slice. The times are simulated.
32 devices in a mesh: grp: 2 (over y), blk: 4 (over z), feat: 4 (over x, core).
Axes of the slice: x: 2, y: 2, z: 4, core: 2. Of those that a mesh axis runs over, the one named last changes fastest.
Arguments:
- queries: bfloat16 [512, 4096], P(('grp', 'blk'), 'feat'), parts along dimension 0, may hold values from -6 to 6
- inv_gram: bfloat16 [4096, 4096], P('feat', 'blk'), may hold values from -0.09375 to 0.09375
- store: bfloat16 [4096, 4096], P(('grp', 'blk'), 'feat'), parts along dimension 0, may hold values from -0.09375 to 0.09375
- example_ids: int32 [2048], P(('grp', 'blk')), parts along dimension 0, may hold values from 0 to 511
- example_weights: float32 [2048], P(('grp', 'blk')), parts along dimension 0, may hold values from 0.2 to 1
- domain_mask: int32 [8, 4], P('grp', 'blk'), parts along dimension 0, may hold values from 0 to 1, as said below
Outputs:
- scores: float32 [4, 128, 1024], P(None, ('grp', 'feat'), 'blk'), parts along dimension 1
There are 2 independent parts, one for each index of `grp`. A program takes and returns all parts, laid end to end along the dimension named above; an argument that names none is the same for every part. Nothing has to cross between parts.
Inputs may be any that keep to these rules, and one draw needn't show every extreme that they name: `domain_mask`: each example block is scored against at least one query block.
All inputs are finite; a program needn't handle non-finite values.
Results may differ from a plain program's by a relative error of at most 0.015.
Values may be sent and summed in bfloat16 or wider, within the bound.
A program may use at most 64 MiB of HBM per device.

v0:
```python
import jax
import jax.numpy as jnp
from jax import lax
from jax.sharding import PartitionSpec as P


def shifted(x, axis, by):
    devices = lax.axis_size(axis)
    return lax.ppermute(x, axis, [(i, (i + by) % devices) for i in range(devices)])


def contract(left, right):
    return lax.dot_general(
        left, right, (((1,), (1,)), ((), ())), preferred_element_type=jnp.float32
    )


def per_device(queries, inv_gram, store, example_ids, example_weights, domain_mask):
    blocks = lax.axis_size("blk")
    own_block = lax.axis_index("blk")
    partial_value = jnp.dot(
        queries,
        lax.all_gather(inv_gram, "blk", axis=1, tiled=True),
        preferred_element_type=jnp.float32,
    )
    precond = lax.psum_scatter(
        partial_value.astype(jnp.bfloat16), "feat", scatter_dimension=1, tiled=True
    )
    examples = jnp.take(store, example_ids, axis=0)

    def make_tile(block):
        value = contract(block, examples)
        value = lax.optimization_barrier(value.astype(jnp.bfloat16)).astype(jnp.float32)
        return value

    def place(collected, block, source):
        return lax.dynamic_update_index_in_dim(collected, make_tile(block), source, 0)

    def forward(block):
        return shifted(block, "blk", 1)

    first = make_tile(precond)
    collected = jnp.zeros((blocks,) + first.shape, jnp.float32)
    collected = lax.dynamic_update_index_in_dim(collected, first, own_block, 0)

    def one_step(offset, carry):
        ahead, gathered = carry
        ahead = forward(ahead)
        return (ahead, place(gathered, ahead, (own_block - offset) % blocks))

    ahead, collected = lax.fori_loop(1, blocks, one_step, (precond, collected))
    summed = lax.psum_scatter(
        collected.astype(jnp.bfloat16), "feat", scatter_dimension=1, tiled=True
    ).astype(jnp.float32)
    factor = domain_mask[:, :, None].astype(jnp.float32)
    return summed * factor * example_weights[None, None, :]


def solution(mesh):
    in_specs = (
        P(("grp", "blk"), "feat"),
        P("feat", "blk"),
        P(("grp", "blk"), "feat"),
        P(("grp", "blk")),
        P(("grp", "blk")),
        P("grp", "blk"),
    )
    out_specs = P(None, ("grp", "feat"), "blk")
    return jax.shard_map(
        per_device, mesh=mesh, in_specs=in_specs, out_specs=out_specs, check_vma=False
    )
```

profile of v0, /device:TPU:0, one launch (start us, length us, event | category | flops | bytes accessed | tf_op | source)
XLA Modules:
  0.0 238.2 jit_solution(8922901721960847313)
XLA Ops:
  6.5 0.0 copy-start
  6.5 0.0 all-gather.2.cloned.1.call-start
  6.5 0.7 all-gather.2.cloned.1.call-update
  7.3 0.0 copy-start.3
  7.3 0.0 reduce-scatter.3.cloned.1.call-start
  7.3 154.0 %all-gather.2.cloned.1.call-done = bf16[1024,4096]{1,0:T(8,128)(2,1)} async-done(((bf16[1024,1024]{1,0:T(8,128)(2,1)}), bf16[1024,4096]{1,0:T(8,128)(2,1)}) %all-gather.2.cloned.1.call-update) | async-done | bytes 8388624 | tf_op jit(solution)/shard_map/all_gather | solution.py:23
  161.3 5.9 %convolution_convert_fusion.1 = bf16[64,4096]{1,0:T(8,128)(2,1)} fusion(bf16[64,1024]{1,0:T(8,128)(2,1)} %param.8, bf16[1024,4096]{1,0:T(8,128)(2,1)} %all-gather.2.cloned.1.call-done), kind=kOutput, calls=%fused_computation.3 | convolution fusion | flops 537133056 | bytes 9043968 | tf_op jit(solution)/shard_map/dot_general | solution.py:21
  167.2 0.0 copy-start.4
  167.2 0.0 copy-start.2
  167.2 0.0 reduce-scatter.3.cloned.1.call-update
  167.2 0.0 reduce-scatter.5.cloned.1.call-start
  167.3 0.0 copy-done.3
  167.3 0.0 copy-done
  167.3 1.2 gather_fusion
  168.5 0.1 broadcast_select_fusion
  168.6 18.6 %reduce-scatter.3.cloned.1.call-done = bf16[64,1024]{1,0:T(8,128)(2,1)} async-done(((bf16[64,4096]{1,0:T(8,128)(2,1)}), bf16[64,1024]{1,0:T(8,128)(2,1)}) %reduce-scatter.3.cloned.1.call-update) | async-done | bytes 131088 | tf_op jit(solution)/shard_map/reduce_scatter | solution.py:26
  187.2 1.2 convolution_convert_fusion.2
  188.4 24.1 %while.17 = (s32[]{:T(128)}, bf16[64,1024]{1,0:T(8,128)(2,1)}, bf16[4,64,256]{2,1,0:T(8,128)(2,1)S(1)}, bf16[256,1024]{1,0:T(8,128)(2,1)S(1)}, s32[]{:T(128)}, /*index=5*/s32[]{:T(128)}, s32[]{:T(128)}, s32[]{:T(128)}, s32[]{:T(128)}) while((s32[]{:T(128)}, bf16[64,1024]{1,0:T(8,128)(2,1)}, bf16[4,64,256]{2,1,0:T(8,128)(2,1)S(1)}, ...), condition=%wide.region_2.3_spmd, body=%wide.region_1.2_spmd.sunk | while | flops 33587216 | bytes 1573156 | solution.py:51
  188.4 1.5 collective-permute-start
  190.0 5.7 %collective-permute-done = bf16[64,1024]{1,0:T(8,128)(2,1)S(1)} collective-permute-done((bf16[64,1024]{1,0:T(8,128)(2,1)}, bf16[64,1024]{1,0:T(8,128)(2,1)S(1)}, u32[]{:S(2)}, u32[]{:S(2)}) %collective-permute-start) | collective-permute-done | bytes 131104 | tf_op jit(solution)/shard_map/while/body/eval_jaxpr/ppermute | solution.py:9
  195.7 0.3 convolution_convert_fusion.4
  196.0 0.6 copy.16
  196.7 0.0 collective-permute-start
  196.7 7.0 %collective-permute-done = bf16[64,1024]{1,0:T(8,128)(2,1)S(1)} collective-permute-done((bf16[64,1024]{1,0:T(8,128)(2,1)}, bf16[64,1024]{1,0:T(8,128)(2,1)S(1)}, u32[]{:S(2)}, u32[]{:S(2)}) %collective-permute-start) | collective-permute-done | bytes 131104 | tf_op jit(solution)/shard_map/while/body/eval_jaxpr/ppermute | solution.py:9
  203.6 0.3 convolution_convert_fusion.4
  203.9 0.6 copy.16
  204.6 0.0 collective-permute-start
  204.6 7.0 %collective-permute-done = bf16[64,1024]{1,0:T(8,128)(2,1)S(1)} collective-permute-done((bf16[64,1024]{1,0:T(8,128)(2,1)}, bf16[64,1024]{1,0:T(8,128)(2,1)S(1)}, u32[]{:S(2)}, u32[]{:S(2)}) %collective-permute-start) | collective-permute-done | bytes 131104 | tf_op jit(solution)/shard_map/while/body/eval_jaxpr/ppermute | solution.py:9
  211.6 0.3 convolution_convert_fusion.4
  211.9 0.6 copy.16
  212.5 0.0 copy-start.1
  212.5 0.6 copy-done.1
  213.1 0.0 reduce-scatter.5.cloned.1.call-update
  213.2 0.0 copy-done.4
  213.2 17.0 %reduce-scatter.5.cloned.1.call-done = bf16[4,16,256]{2,1,0:T(8,128)(2,1)} async-done(((bf16[4,64,256]{2,1,0:T(8,128)(2,1)}), bf16[4,16,256]{2,1,0:T(8,128)(2,1)}) %reduce-scatter.5.cloned.1.call-update) | async-done | bytes 32784 | tf_op jit(solution)/shard_map/reduce_scatter | solution.py:52
  230.2 0.0 copy-done.2
  230.2 1.5 multiply_multiply_fusion
  (9 shorter events, 0.1 us)
Async XLA Ops:
  6.5 160.8 %copy-start = (bf16[512,1024]{1,0:T(8,128)(2,1)S(1)}, bf16[512,1024]{1,0:T(8,128)(2,1)}, u32[]{:S(2)}) copy-start(bf16[512,1024]{1,0:T(8,128)(2,1)} %param.10) | copy-start | bytes 3145732
  6.5 154.8 %all-gather.2.cloned.1.call-start = ((), (), s32[]{:S(2)}) async-start(), calls=%async_computation.2 | async-start | bytes 10485760 | tf_op jit(solution)/shard_map/all_gather | solution.py:23
  7.3 160.0 %copy-start.3 = (s32[256]{0:T(256)S(1)}, s32[256]{0:T(256)}, u32[]{:S(2)}) copy-start(s32[256]{0:T(256)} %param.11) | copy-start | bytes 3076
  7.3 179.9 %reduce-scatter.3.cloned.1.call-start = ((), (), s32[]{:S(2)}) async-start(), calls=%async_computation.3 | async-start | bytes 655360 | tf_op jit(solution)/shard_map/reduce_scatter | solution.py:26
  167.2 46.0 %copy-start.4 = (s32[4,1]{0,1:T(1,128)S(1)}, s32[4,1]{0,1:T(1,128)}, u32[]{:S(2)}) copy-start(s32[4,1]{0,1:T(1,128)} %param.13) | copy-start | bytes 52
  167.2 63.0 %copy-start.2 = (f32[256]{0:T(256)S(1)}, f32[256]{0:T(256)}, u32[]{:S(2)}) copy-start(f32[256]{0:T(256)} %param.12) | copy-start | bytes 3076
  167.2 63.0 %reduce-scatter.5.cloned.1.call-start = ((), (), s32[]{:S(2)}) async-start(), calls=%async_computation.4 | async-start | bytes 163840 | tf_op jit(solution)/shard_map/reduce_scatter | solution.py:52
  188.4 7.3 %collective-permute-start = (bf16[64,1024]{1,0:T(8,128)(2,1)}, bf16[64,1024]{1,0:T(8,128)(2,1)S(1)}, u32[]{:S(2)}, u32[]{:S(2)}) collective-permute-start(bf16[64,1024]{1,0:T(8,128)(2,1)} %get-tuple-element.190), channel_id=1, source_target_pairs={{0,4},{4,8},{8,12},{12,0},{1,5},{5,9},{9,13},{13,1},{2,6},{6,10},{... | collective-permute-start | bytes 393224 | tf_op jit(solution)/shard_map/while/body/eval_jaxpr/ppermute | solution.py:9
  196.7 7.0 %collective-permute-start = (bf16[64,1024]{1,0:T(8,128)(2,1)}, bf16[64,1024]{1,0:T(8,128)(2,1)S(1)}, u32[]{:S(2)}, u32[]{:S(2)}) collective-permute-start(bf16[64,1024]{1,0:T(8,128)(2,1)} %get-tuple-element.190), channel_id=1, source_target_pairs={{0,4},{4,8},{8,12},{12,0},{1,5},{5,9},{9,13},{13,1},{2,6},{6,10},{... | collective-permute-start | bytes 393224 | tf_op jit(solution)/shard_map/while/body/eval_jaxpr/ppermute | solution.py:9
  204.6 7.0 %collective-permute-start = (bf16[64,1024]{1,0:T(8,128)(2,1)}, bf16[64,1024]{1,0:T(8,128)(2,1)S(1)}, u32[]{:S(2)}, u32[]{:S(2)}) collective-permute-start(bf16[64,1024]{1,0:T(8,128)(2,1)} %get-tuple-element.190), channel_id=1, source_target_pairs={{0,4},{4,8},{8,12},{12,0},{1,5},{5,9},{9,13},{13,1},{2,6},{6,10},{... | collective-permute-start | bytes 393224 | tf_op jit(solution)/shard_map/while/body/eval_jaxpr/ppermute | solution.py:9
  212.5 0.6 copy-start.1
Sparse Core Ops, SparseCore 0:
  8.9 152.3 all-gather.1
  167.3 19.8 reduce-scatter.2
  213.3 16.8 reduce-scatter.4
where the time goes:
time: 238 us
  waiting for transfers between devices  210 us (88%)
  between operations  13.2 us (6%)
  matrix products  7.91 us (3%)
  local copies, waits for them, and re-layouts  3.77 us (2%)
    all_gather x1, waiting for transfers between devices, per_device(): lax.all_gather(inv_gram, 'blk', axis=1, tiled=True)  154 us
    ppermute x3, waiting for transfers between devices, shifted(): lax.ppermute(x, axis, [(i, (i + by) % devices) for i in range(devices)])  19.7 us
    reduce_scatter x1, waiting for transfers between devices, per_device(): lax.psum_scatter(partial_value.astype(jnp.bfloat16), 'feat', scatter_dime...  18.6 us
    reduce_scatter x1, waiting for transfers between devices, per_device(): lax.psum_scatter(collected.astype(jnp.bfloat16), 'feat', scatter_dimensio...  17 us
    dot_general x1, matrix products, per_device(): jnp.dot(queries, lax.all_gather(inv_gram, 'blk', axis=1, tiled=True), pre...  5.87 us
  transfers between devices with their start and end apart: 6, of which 6 were waited for; matrix products, arithmetic and copies ran while one was open for 1% of the time, Pallas kernels for 0%

commit v1 on v0

v1 whole, which is shorter than its diff:
```python
import functools

import jax
import jax.numpy as jnp
from jax import lax
from jax.experimental import pallas as pl
from jax.experimental.pallas import tpu as pltpu
from jax.sharding import PartitionSpec as P

MESH = pl.DeviceIdType.MESH


def contract(left, right):
    return lax.dot_general(
        left, right, (((1,), (1,)), ((), ())), preferred_element_type=jnp.float32
    )


def kernel(
    n_blk,
    n_feat,
    q_hbm,
    g_hbm,
    store_hbm,
    ids_ref,
    out_ref,
    q_all,
    gram,
    stored,
    e_all,
    p_send,
    p_recv,
    cond,
    local_sem,
    a_send,
    a_recv,
    e_send,
    e_recv,
    b_send,
    b_recv,
    c_send,
    c_recv,
):
    z = lax.axis_index("blk")
    f = lax.axis_index("feat")
    half = z // 2
    order = [z, 1 + 4 * half - z, 2 - half, 3 - 3 * half]
    sibling = f + 1 - 2 * (f % 2)
    across = (f + 2) % 4

    load_q = pltpu.make_async_copy(q_hbm, q_all.at[z], local_sem.at[0])
    load_g = pltpu.make_async_copy(g_hbm, gram, local_sem.at[1])
    load_s = pltpu.make_async_copy(store_hbm, stored, local_sem.at[2])
    load_q.start()
    load_g.start()
    load_s.start()

    def send(src, dst, send_sem, recv_sem, target):
        return pltpu.make_async_remote_copy(
            src_ref=src,
            dst_ref=dst,
            send_sem=send_sem,
            recv_sem=recv_sem,
            device_id=target,
            device_id_type=MESH,
        )

    barrier = pltpu.get_barrier_semaphore()
    for d in range(1, n_blk):
        pl.semaphore_signal(
            barrier, inc=1, device_id={"blk": (z + d) % n_blk}, device_id_type=MESH
        )
    for d in range(1, n_feat):
        pl.semaphore_signal(
            barrier, inc=1, device_id={"feat": (f + d) % n_feat}, device_id_type=MESH
        )
    pl.semaphore_wait(barrier, n_blk + n_feat - 2)

    def a_copy(j, target):
        return send(
            q_all.at[j], q_all.at[j], a_send.at[target], a_recv.at[j], {"blk": target}
        )

    def b_copy(j, src, target):
        return send(
            p_send.at[j, target],
            p_recv.at[j, src],
            b_send.at[j, target],
            b_recv.at[j, src],
            {"feat": target},
        )

    def c_copy(c, j, target):
        return send(
            cond.at[c, j],
            cond.at[c, j],
            c_send.at[j, target],
            c_recv.at[c, j],
            {"blk": target},
        )

    def e_copy(src, slot, target):
        return send(
            e_all.at[src], e_all.at[src], e_send.at[slot], e_recv.at[src], {"feat": target}
        )

    load_q.wait()
    for s in range(1, n_blk):
        a_copy(z, order[s]).start()

    def multiply(s):
        j = order[s]
        if s > 0:
            a_copy(j, z).wait_recv()
        value = jnp.dot(q_all[j], gram[...], preferred_element_type=jnp.float32)
        rows = value.shape[0] // n_feat
        p_send[j] = value.astype(jnp.bfloat16).reshape(n_feat, rows, value.shape[1])
        for d in range(1, n_feat):
            b_copy(j, f, (f + d) % n_feat).start()

    def finish(s):
        j = order[s]
        total = p_send[j, f].astype(jnp.float32)
        for d in range(1, n_feat):
            src = (f + d) % n_feat
            b_copy(j, src, f).wait_recv()
            total = total + p_recv[j, src].astype(jnp.float32)
        cond[z, j] = total.astype(jnp.bfloat16)
        for t in range(1, n_blk):
            c_copy(z, j, order[t]).start()

    load_g.wait()
    multiply(0)

    load_s.wait()
    held = stored.shape[0]
    examples = ids_ref.shape[1]
    pick = jnp.where(
        lax.broadcasted_iota(jnp.int32, (held, examples), 0) == ids_ref[...], 1.0, 0.0
    ).astype(jnp.bfloat16)
    e_all[f] = lax.dot_general(
        pick, stored[...], (((0,), (0,)), ((), ())), preferred_element_type=jnp.float32
    ).astype(jnp.bfloat16)
    e_copy(f, 0, across).start()
    e_copy(f, 1, sibling).start()

    finish(0)
    multiply(1)
    finish(1)
    multiply(2)
    finish(2)
    multiply(3)
    e_copy(across, 2, f).wait_recv()
    e_copy(across, 2, sibling).start()
    finish(3)
    e_copy(sibling, 1, f).wait_recv()
    e_copy((sibling + 2) % 4, 1, f).wait_recv()

    total = None
    for s in range(n_blk):
        c = order[s]
        if s > 0:
            for t in range(n_blk):
                c_copy(c, order[t], z).wait_recv()
        rows = cond.shape[1] * cond.shape[2]
        value = contract(cond[c].reshape(rows, cond.shape[3]), e_all[c])
        total = value if total is None else total + value
    out_ref[...] = total.reshape(out_ref.shape)

    for s in range(1, n_blk):
        a_copy(z, order[s]).wait_send()
    for j in range(n_blk):
        for d in range(1, n_feat):
            b_copy(j, f, (f + d) % n_feat).wait_send()
        for s in range(1, n_blk):
            c_copy(z, j, order[s]).wait_send()
    for slot in range(3):
        e_copy(f, slot, sibling).wait_send()


def fused(n_blk, n_feat, queries, inv_gram, store, ids):
    qdev, width = queries.shape
    edev = ids.shape[1]
    rows = qdev // n_feat
    dma = pltpu.SemaphoreType.DMA
    any_spec = pl.BlockSpec(memory_space=pl.ANY)
    vmem_spec = pl.BlockSpec(memory_space=pltpu.VMEM)
    return pl.pallas_call(
        functools.partial(kernel, n_blk, n_feat),
        out_shape=jax.ShapeDtypeStruct((n_blk, rows, edev), jnp.float32),
        in_specs=[any_spec, any_spec, any_spec, vmem_spec],
        out_specs=vmem_spec,
        scratch_shapes=[
            pltpu.VMEM((n_blk, qdev, width), jnp.bfloat16),
            pltpu.VMEM(inv_gram.shape, jnp.bfloat16),
            pltpu.VMEM(store.shape, jnp.bfloat16),
            pltpu.VMEM((n_feat, edev, width), jnp.bfloat16),
            pltpu.VMEM((n_blk, n_feat, rows, inv_gram.shape[1]), jnp.bfloat16),
            pltpu.VMEM((n_blk, n_feat, rows, inv_gram.shape[1]), jnp.bfloat16),
            pltpu.VMEM((n_blk, n_blk, rows, inv_gram.shape[1]), jnp.bfloat16),
            dma((3,)),
            dma((n_blk,)),
            dma((n_blk,)),
            dma((3,)),
            dma((n_feat,)),
            dma((n_blk, n_feat)),
            dma((n_blk, n_feat)),
            dma((n_blk, n_blk)),
            dma((n_blk, n_blk)),
        ],
        compiler_params=pltpu.CompilerParams(
            collective_id=0, has_side_effects=True, vmem_limit_bytes=40 * 1024 * 1024
        ),
    )(queries, inv_gram, store, ids)


def plain(n_blk, n_feat, queries, inv_gram, store, ids):
    gathered = lax.all_gather(queries, "blk", axis=0, tiled=True)
    partial_value = jnp.dot(gathered, inv_gram, preferred_element_type=jnp.float32)
    rows = queries.shape[0] // n_feat
    spread = partial_value.astype(jnp.bfloat16).reshape(n_blk, n_feat, rows, -1)
    precond = lax.psum_scatter(spread, "feat", scatter_dimension=1, tiled=True)
    precond = lax.all_gather(
        precond.reshape(n_blk * rows, -1), "blk", axis=1, tiled=True
    )
    examples = lax.all_gather(
        jnp.take(store, ids[0], axis=0), "feat", axis=1, tiled=True
    )
    return contract(precond, examples).reshape(n_blk, rows, -1)


def per_device(queries, inv_gram, store, example_ids, example_weights, domain_mask):
    n_blk, n_feat = lax.axis_size("blk"), lax.axis_size("feat")
    lines = n_blk == 4 and n_feat == 4
    aligned = queries.shape[0] % (16 * n_feat) == 0 and queries.shape[1] % 128 == 0
    same = queries.shape[1] == inv_gram.shape[1]
    score = fused if lines and aligned and same else plain
    raw = score(n_blk, n_feat, queries, inv_gram, store, example_ids[None, :])
    factor = domain_mask[:, :, None].astype(jnp.float32)
    return raw * factor * example_weights[None, None, :]


def solution(mesh):
    in_specs = (
        P(("grp", "blk"), "feat"),
        P("feat", "blk"),
        P(("grp", "blk"), "feat"),
        P(("grp", "blk")),
        P(("grp", "blk")),
        P("grp", "blk"),
    )
    out_specs = P(None, ("grp", "feat"), "blk")
    return jax.shard_map(
        per_device, mesh=mesh, in_specs=in_specs, out_specs=out_specs, check_vma=False
    )
```

time: 238 us -> 40.6 us (0.17)
  waiting for transfers between devices: 210 us -> 0 us
  Pallas kernels: 0 us -> 34.6 us
  between operations: 13.2 us -> 0.02 us
  matrix products: 7.91 us -> 0 us
    all_gather x1 -> x0, waiting for transfers between devices: 154 us -> none  [per_device(): lax.all_gather(inv_gram, 'blk', axis=1, tiled=True)]
    reduce_scatter x2 -> x0, waiting for transfers between devices: 35.6 us -> none  [the longest x1 18.6 us: per_device(): lax.psum_scatter(partial_value.astype(jnp.bfloat16), 'feat', scatter_dime...]
    pallas_call x0 -> x1, Pallas kernels: none -> 34.6 us  [fused(): pl.pallas_call(functools.partial(kernel, n_blk, n_feat), out_shape=jax.Sh...]
    ppermute x3 -> x0, waiting for transfers between devices: 19.7 us -> none  [shifted(): lax.ppermute(x, axis, [(i, (i + by) % devices) for i in range(devices)])]
    dot_general x5 -> x0, matrix products: 7.91 us -> none  [the longest x1 5.87 us: per_device(): jnp.dot(queries, lax.all_gather(inv_gram, 'blk', axis=1, tiled=True), pre...]
    unnamed x10, local copies, waits for them, and re-layouts: 0.66 us -> 4.4 us
  transfers between devices with their start and end apart: 6 -> 0, of which waited for: 6 -> 0; matrix products, arithmetic and copies ran while one was open for 1% -> 0% of each run, Pallas kernels for 0% -> 0%
where the time goes in v1:
time: 40.6 us; the launch traced here: 40.4 us
  Pallas kernels  34.6 us (85%)
  local copies, waits for them, and re-layouts  4.4 us (11%)
  other arithmetic  1.38 us (3%)
    pallas_call x1, Pallas kernels, fused(): pl.pallas_call(functools.partial(kernel, n_blk, n_feat), out_shape=jax.Sh...  34.6 us
    unnamed x10, local copies, waits for them, and re-layouts  4.4 us

profile of v1, /device:TPU:0, one launch (start us, length us, event | category | flops | bytes accessed | tf_op | source)
XLA Modules:
  0.0 40.4 jit_solution(17575014947871358831)
XLA Ops:
  0.0 0.0 copy-start.4
  0.0 0.7 %convert_bitcast_fusion = f32[4]{0:T(128)S(1)} fusion(s32[4,1]{0,1:T(1,128)} %param.11), kind=kLoop, calls=%fused_computation.1 | loop fusion | flops 4 | bytes 32 | tf_op jit(solution)/shard_map/convert_element_type | solution.py:239
  0.7 0.0 copy-start
  0.7 1.6 %copy-done = bf16[1024,1024]{1,0:T(8,128)(2,1)S(1)} copy-done((bf16[1024,1024]{1,0:T(8,128)(2,1)S(1)}, bf16[1024,1024]{1,0:T(8,128)(2,1)}, u32[]{:S(2)}) %copy-start) | copy-done | bytes 2097176
  2.3 0.0 copy-start.1
  2.3 1.2 %copy-done.1 = bf16[512,1024]{1,0:T(8,128)(2,1)S(1)} copy-done((bf16[512,1024]{1,0:T(8,128)(2,1)S(1)}, bf16[512,1024]{1,0:T(8,128)(2,1)}, u32[]{:S(2)}) %copy-start.1) | copy-done | bytes 1048600
  3.5 0.0 copy-start.2
  3.5 0.9 %copy-done.2 = bf16[64,1024]{1,0:T(8,128)(2,1)S(1)} copy-done((bf16[64,1024]{1,0:T(8,128)(2,1)S(1)}, bf16[64,1024]{1,0:T(8,128)(2,1)}, u32[]{:S(2)}) %copy-start.2) | copy-done | bytes 131096
  4.4 0.0 copy-start.3
  4.4 0.7 %copy-done.3 = s32[256]{0:T(256)S(1)} copy-done((s32[256]{0:T(256)S(1)}, s32[256]{0:T(256)}, u32[]{:S(2)}) %copy-start.3) | copy-done | bytes 1048
  5.1 34.6 %shard_map.64 = f32[4,16,256]{2,1,0:T(8,128)S(1)} custom-call(bf16[64,1024]{1,0:T(8,128)(2,1)S(1)} %copy-done.2, bf16[1024,1024]{1,0:T(8,128)(2,1)S(1)} %copy-done, bf16[512,1024]{1,0:T(8,128)(2,1)S(1)} %copy-done.1, s32[1,256]{1,0:T(1,128)S(1)} %bitcast.3), custom_call_target="tpu_custom_call" | custom-call | tf_op jit(solution)/shard_map/pallas_call | solution.py:188
  39.7 0.0 copy-done.4
  39.7 0.7 %multiply_multiply_fusion = f32[4,16,256]{2,1,0:T(8,128)} fusion(f32[4,16,256]{2,1,0:T(8,128)S(1)} %shard_map.64, f32[256]{0:T(256)S(1)} %copy-done.4, f32[4]{0:T(128)S(1)} %convert_bitcast_fusion), kind=kLoop, calls=%fused_computation | loop fusion | flops 32768 | bytes 132112 | tf_op jit(solution)/shard_map/mul | solution.py:240
Async XLA Ops:
  0.0 39.7 %copy-start.4 = (f32[256]{0:T(256)S(1)}, f32[256]{0:T(256)}, u32[]{:S(2)}) copy-start(f32[256]{0:T(256)} %param.10) | copy-start | bytes 3076
  0.7 1.6 %copy-start = (bf16[1024,1024]{1,0:T(8,128)(2,1)S(1)}, bf16[1024,1024]{1,0:T(8,128)(2,1)}, u32[]{:S(2)}) copy-start(bf16[1024,1024]{1,0:T(8,128)(2,1)} %g_hbm.1) | copy-start | bytes 6291460
  2.3 1.2 %copy-start.1 = (bf16[512,1024]{1,0:T(8,128)(2,1)S(1)}, bf16[512,1024]{1,0:T(8,128)(2,1)}, u32[]{:S(2)}) copy-start(bf16[512,1024]{1,0:T(8,128)(2,1)} %store_hbm.1) | copy-start | bytes 3145732
  3.5 0.9 %copy-start.2 = (bf16[64,1024]{1,0:T(8,128)(2,1)S(1)}, bf16[64,1024]{1,0:T(8,128)(2,1)}, u32[]{:S(2)}) copy-start(bf16[64,1024]{1,0:T(8,128)(2,1)} %q_hbm.1) | copy-start | bytes 393220
  4.4 0.7 %copy-start.3 = (s32[256]{0:T(256)S(1)}, s32[256]{0:T(256)}, u32[]{:S(2)}) copy-start(s32[256]{0:T(256)} %param.9) | copy-start | bytes 3076

commit v2 on v1

--- a/solution.py
+++ b/solution.py
@@ -8,6 +8,7 @@
 from jax.sharding import PartitionSpec as P
 
 MESH = pl.DeviceIdType.MESH
+VMEM = 63 * 1024 * 1024
 
 
 def contract(left, right):
@@ -22,8 +23,11 @@
     q_hbm,
     g_hbm,
     store_hbm,
+    ids_hbm,
+    mask_hbm,
+    out_ref,
     ids_ref,
-    out_ref,
+    mask_ref,
     q_all,
     gram,
     stored,
@@ -45,15 +49,16 @@
     f = lax.axis_index("feat")
     half = z // 2
     order = [z, 1 + 4 * half - z, 2 - half, 3 - 3 * half]
+    near, middle, far = order[1], order[2], order[3]
+    between = (z - 1) * (z - 2) == 0
     sibling = f + 1 - 2 * (f % 2)
     across = (f + 2) % 4
 
     load_q = pltpu.make_async_copy(q_hbm, q_all.at[z], local_sem.at[0])
     load_g = pltpu.make_async_copy(g_hbm, gram, local_sem.at[1])
     load_s = pltpu.make_async_copy(store_hbm, stored, local_sem.at[2])
-    load_q.start()
-    load_g.start()
-    load_s.start()
+    load_ids = pltpu.make_async_copy(ids_hbm, ids_ref, local_sem.at[3])
+    load_mask = pltpu.make_async_copy(mask_hbm, mask_ref, local_sem.at[4])
 
     def send(src, dst, send_sem, recv_sem, target):
         return pltpu.make_async_remote_copy(
@@ -74,11 +79,19 @@
         pl.semaphore_signal(
             barrier, inc=1, device_id={"feat": (f + d) % n_feat}, device_id_type=MESH
         )
-    pl.semaphore_wait(barrier, n_blk + n_feat - 2)
-
-    def a_copy(j, target):
+    load_q.start()
+    load_g.start()
+    load_ids.start()
+    load_s.start()
+    load_mask.start()
+
+    def a_copy(j, target, slot, src=None):
         return send(
-            q_all.at[j], q_all.at[j], a_send.at[target], a_recv.at[j], {"blk": target}
+            q_all.at[j] if src is None else src,
+            q_all.at[j],
+            a_send.at[slot],
+            a_recv.at[j],
+            {"blk": target},
         )
 
     def b_copy(j, src, target):
@@ -90,11 +103,11 @@
             {"feat": target},
         )
 
-    def c_copy(c, j, target):
+    def c_copy(c, j, target, slot):
         return send(
             cond.at[c, j],
             cond.at[c, j],
-            c_send.at[j, target],
+            c_send.at[j, slot],
             c_recv.at[c, j],
             {"blk": target},
         )
@@ -104,19 +117,22 @@
             e_all.at[src], e_all.at[src], e_send.at[slot], e_recv.at[src], {"feat": target}
         )
 
-    load_q.wait()
-    for s in range(1, n_blk):
-        a_copy(z, order[s]).start()
-
     def multiply(s):
         j = order[s]
         if s > 0:
-            a_copy(j, z).wait_recv()
+            a_copy(j, z, 0).wait_recv()
+        if s >= 2:
+            @pl.when(between)
+            def _():
+                a_copy(j, near, s).start()
+
         value = jnp.dot(q_all[j], gram[...], preferred_element_type=jnp.float32)
         rows = value.shape[0] // n_feat
         p_send[j] = value.astype(jnp.bfloat16).reshape(n_feat, rows, value.shape[1])
+
+    def spread(s):
         for d in range(1, n_feat):
-            b_copy(j, f, (f + d) % n_feat).start()
+            b_copy(order[s], f, (f + d) % n_feat).start()
 
     def finish(s):
         j = order[s]
@@ -126,12 +142,34 @@
             b_copy(j, src, f).wait_recv()
             total = total + p_recv[j, src].astype(jnp.float32)
         cond[z, j] = total.astype(jnp.bfloat16)
-        for t in range(1, n_blk):
-            c_copy(z, j, order[t]).start()
-
+        c_copy(z, j, near, 0).start()
+        c_copy(z, j, middle, 1).start()
+
+        @pl.when(between)
+        def _():
+            c_copy(z, j, far, 2).start()
+
+    def hand_on(t):
+        j = 3 - 3 * half + t * (2 * half - 1)
+
+        @pl.when(between)
+        def _():
+            c_copy(far, j, z, 0).wait_recv()
+            c_copy(far, j, near, 3).start()
+
+
+    pl.semaphore_wait(barrier, n_blk + n_feat - 2)
+    a_copy(z, near, 0, q_hbm).start()
+
+    @pl.when(between)
+    def _():
+        a_copy(z, middle, 1, q_hbm).start()
+
+    load_q.wait()
     load_g.wait()
     multiply(0)
-
+    spread(0)
+    load_ids.wait()
     load_s.wait()
     held = stored.shape[0]
     examples = ids_ref.shape[1]
@@ -144,41 +182,74 @@
     e_copy(f, 0, across).start()
     e_copy(f, 1, sibling).start()
 
+    @pl.when(jnp.logical_not(between))
+    def _():
+        a_copy(z, near, 0, q_hbm).wait_send()
+        a_copy(z, middle, 1, q_hbm).start()
+
     finish(0)
     multiply(1)
+    spread(1)
     finish(1)
     multiply(2)
+    spread(2)
+    hand_on(0)
     finish(2)
     multiply(3)
+    spread(3)
+    hand_on(1)
+    finish(3)
+    hand_on(2)
+    hand_on(3)
     e_copy(across, 2, f).wait_recv()
     e_copy(across, 2, sibling).start()
-    finish(3)
     e_copy(sibling, 1, f).wait_recv()
     e_copy((sibling + 2) % 4, 1, f).wait_recv()
 
     total = None
     for s in range(n_blk):
         c = order[s]
-        if s > 0:
-            for t in range(n_blk):
-                c_copy(c, order[t], z).wait_recv()
+        if 0 < s < 3:
+            for j in range(n_blk):
+                c_copy(c, j, z, 0).wait_recv()
+        if s == 3:
+
+            @pl.when(jnp.logical_not(between))
+            def _():
+                for j in range(n_blk):
+                    c_copy(c, j, z, 0).wait_recv()
+
         rows = cond.shape[1] * cond.shape[2]
         value = contract(cond[c].reshape(rows, cond.shape[3]), e_all[c])
         total = value if total is None else total + value
-    out_ref[...] = total.reshape(out_ref.shape)
-
-    for s in range(1, n_blk):
-        a_copy(z, order[s]).wait_send()
+    load_mask.wait()
+    total = total.reshape(out_ref.shape)
+    for j in range(n_blk):
+        out_ref[j] = total[j] * mask_ref[0, j].astype(jnp.float32)
+
     for j in range(n_blk):
         for d in range(1, n_feat):
             b_copy(j, f, (f + d) % n_feat).wait_send()
-        for s in range(1, n_blk):
-            c_copy(z, j, order[s]).wait_send()
+        c_copy(z, j, near, 0).wait_send()
+        c_copy(z, j, middle, 1).wait_send()
+
+    @pl.when(between)
+    def _():
+        for slot in range(4):
+            a_copy(z, near, slot).wait_send()
+        for j in range(n_blk):
+            c_copy(z, j, far, 2).wait_send()
+            c_copy(far, j, near, 3).wait_send()
+
+    @pl.when(jnp.logical_not(between))
+    def _():
+        a_copy(z, middle, 1).wait_send()
+
     for slot in range(3):
         e_copy(f, slot, sibling).wait_send()
 
 
-def fused(n_blk, n_feat, queries, inv_gram, store, ids):
+def fused(n_blk, n_feat, queries, inv_gram, store, ids, mask):
     qdev, width = queries.shape
     edev = ids.shape[1]
     rows = qdev // n_feat
@@ -188,9 +259,11 @@
     return pl.pallas_call(
         functools.partial(kernel, n_blk, n_feat),
         out_shape=jax.ShapeDtypeStruct((n_blk, rows, edev), jnp.float32),
-        in_specs=[any_spec, any_spec, any_spec, vmem_spec],
+        in_specs=[any_spec] * 5,
         out_specs=vmem_spec,
         scratch_shapes=[
+            pltpu.VMEM(ids.shape, jnp.int32),
+            pltpu.SMEM(mask.shape, jnp.int32),
             pltpu.VMEM((n_blk, qdev, width), jnp.bfloat16),
             pltpu.VMEM(inv_gram.shape, jnp.bfloat16),
             pltpu.VMEM(store.shape, jnp.bfloat16),
@@ -198,7 +271,7 @@
             pltpu.VMEM((n_blk, n_feat, rows, inv_gram.shape[1]), jnp.bfloat16),
             pltpu.VMEM((n_blk, n_feat, rows, inv_gram.shape[1]), jnp.bfloat16),
             pltpu.VMEM((n_blk, n_blk, rows, inv_gram.shape[1]), jnp.bfloat16),
-            dma((3,)),
+            dma((5,)),
             dma((n_blk,)),
             dma((n_blk,)),
             dma((3,)),
@@ -209,12 +282,12 @@
             dma((n_blk, n_blk)),
         ],
         compiler_params=pltpu.CompilerParams(
-            collective_id=0, has_side_effects=True, vmem_limit_bytes=40 * 1024 * 1024
+            collective_id=0, has_side_effects=True, vmem_limit_bytes=VMEM
         ),
-    )(queries, inv_gram, store, ids)
-
-
-def plain(n_blk, n_feat, queries, inv_gram, store, ids):
+    )(queries, inv_gram, store, ids, mask)
+
+
+def plain(n_blk, n_feat, queries, inv_gram, store, ids, mask):
     gathered = lax.all_gather(queries, "blk", axis=0, tiled=True)
     partial_value = jnp.dot(gathered, inv_gram, preferred_element_type=jnp.float32)
     rows = queries.shape[0] // n_feat
@@ -226,7 +299,8 @@
     examples = lax.all_gather(
         jnp.take(store, ids[0], axis=0), "feat", axis=1, tiled=True
     )
-    return contract(precond, examples).reshape(n_blk, rows, -1)
+    raw = contract(precond, examples).reshape(n_blk, rows, -1)
+    return raw * mask[0][:, None, None].astype(jnp.float32)
 
 
 def per_device(queries, inv_gram, store, example_ids, example_weights, domain_mask):
@@ -235,9 +309,9 @@
     aligned = queries.shape[0] % (16 * n_feat) == 0 and queries.shape[1] % 128 == 0
     same = queries.shape[1] == inv_gram.shape[1]
     score = fused if lines and aligned and same else plain
-    raw = score(n_blk, n_feat, queries, inv_gram, store, example_ids[None, :])
-    factor = domain_mask[:, :, None].astype(jnp.float32)
-    return raw * factor * example_weights[None, None, :]
+    ids, mask = example_ids[None, :], domain_mask.reshape(1, n_blk)
+    raw = score(n_blk, n_feat, queries, inv_gram, store, ids, mask)
+    return raw * example_weights[None, None, :]
 
 
 def solution(mesh):

time: 40.6 us -> 46.3 us (1.14)
  Pallas kernels: 34.6 us -> 44.6 us
  local copies, waits for them, and re-layouts: 4.4 us -> 0.01 us
    pallas_call x1, Pallas kernels: 34.6 us -> 44.6 us  [fused(): pl.pallas_call(functools.partial(kernel, n_blk, n_feat), out_shape=jax.Sh...]
    unnamed x10 -> x2, local copies, waits for them, and re-layouts: 4.4 us -> 0.01 us
    mul x1, other arithmetic: 0.71 us -> 1.48 us  [per_device(): return raw * example_weights[None, None, :]]
    convert_element_type x1 -> x0, other arithmetic: 0.67 us -> none  [per_device(): factor = domain_mask[:, :, None].astype(jnp.float32)]
where the time goes in v2:
time: 46.3 us; the launch traced here: 46.1 us
  Pallas kernels  44.6 us (96%)
  other arithmetic  1.48 us (3%)
    pallas_call x1, Pallas kernels, fused(): pl.pallas_call(functools.partial(kernel, n_blk, n_feat), out_shape=jax.Sh...  44.6 us
    mul x1, other arithmetic, per_device(): return raw * example_weights[None, None, :]  1.48 us

profile of v2, /device:TPU:0, one launch (start us, length us, event | category | flops | bytes accessed | tf_op | source)
XLA Modules:
  0.0 46.1 jit_solution(1406675689890462136)
XLA Ops:
  0.0 0.0 copy-start
  0.0 44.6 %shard_map.64 = f32[4,16,256]{2,1,0:T(8,128)} custom-call(bf16[64,1024]{1,0:T(8,128)(2,1)} %q_hbm.1, bf16[1024,1024]{1,0:T(8,128)(2,1)} %g_hbm.1, bf16[512,1024]{1,0:T(8,128)(2,1)} %store_hbm.1, s32[1,256]{1,0:T(1,128)} %bitcast.2, s32[1,4]{1,0:T(1,128)} %bitcast.3), custom_call_target="tpu_custom_call" | custom-call | tf_op jit(solution)/shard_map/pallas_call | solution.py:259
  44.6 0.0 copy-done
  44.6 1.5 %broadcast_multiply_fusion = f32[4,16,256]{2,1,0:T(8,128)} fusion(f32[4,16,256]{2,1,0:T(8,128)} %shard_map.64, f32[256]{0:T(256)S(1)} %copy-done), kind=kLoop, calls=%fused_computation | loop fusion | flops 16384 | bytes 132096 | tf_op jit(solution)/shard_map/mul | solution.py:314
Async XLA Ops:
  0.0 44.6 %copy-start = (f32[256]{0:T(256)S(1)}, f32[256]{0:T(256)}, u32[]{:S(2)}) copy-start(f32[256]{0:T(256)} %param.10) | copy-start | bytes 3076

commit v3 on v2

--- a/solution.py
+++ b/solution.py
@@ -9,6 +9,7 @@
 
 MESH = pl.DeviceIdType.MESH
 VMEM = 63 * 1024 * 1024
+PARTS = 4
 
 
 def contract(left, right):
@@ -48,8 +49,9 @@
     z = lax.axis_index("blk")
     f = lax.axis_index("feat")
     half = z // 2
-    order = [z, 1 + 4 * half - z, 2 - half, 3 - 3 * half]
-    near, middle, far = order[1], order[2], order[3]
+    order = [z, z + 1 - 2 * half, 2 - 2 * z + 5 * half, 3 - 3 * half]
+    first, second, far = order[1], order[2], order[3]
+    end = 3 * half
     between = (z - 1) * (z - 2) == 0
     sibling = f + 1 - 2 * (f % 2)
     across = (f + 2) % 4
@@ -112,19 +114,26 @@
             {"blk": target},
         )
 
-    def e_copy(src, slot, target):
+    def e_copy(src, slot, i, target):
+        size = e_all.shape[1] // PARTS
+        part = e_all.at[src, pl.ds(i * size, size)]
         return send(
-            e_all.at[src], e_all.at[src], e_send.at[slot], e_recv.at[src], {"feat": target}
-        )
+            part, part, e_send.at[slot, i], e_recv.at[src, i], {"feat": target}
+        )
+
+    def push_e(i):
+        if i < PARTS:
+            e_copy(f, 0, i, across).start()
+            e_copy(f, 1, i, sibling).start()
 
     def multiply(s):
         j = order[s]
         if s > 0:
             a_copy(j, z, 0).wait_recv()
-        if s >= 2:
+        if s % 2 == 1:
             @pl.when(between)
             def _():
-                a_copy(j, near, s).start()
+                a_copy(j, end, 2 + s // 2).start()
 
         value = jnp.dot(q_all[j], gram[...], preferred_element_type=jnp.float32)
         rows = value.shape[0] // n_feat
@@ -142,28 +151,12 @@
             b_copy(j, src, f).wait_recv()
             total = total + p_recv[j, src].astype(jnp.float32)
         cond[z, j] = total.astype(jnp.bfloat16)
-        c_copy(z, j, near, 0).start()
-        c_copy(z, j, middle, 1).start()
-
-        @pl.when(between)
-        def _():
-            c_copy(z, j, far, 2).start()
-
-    def hand_on(t):
-        j = 3 - 3 * half + t * (2 * half - 1)
-
-        @pl.when(between)
-        def _():
-            c_copy(far, j, z, 0).wait_recv()
-            c_copy(far, j, near, 3).start()
-
+        for t in (3, 2, 1):
+            c_copy(z, j, order[t], t - 1).start()
 
     pl.semaphore_wait(barrier, n_blk + n_feat - 2)
-    a_copy(z, near, 0, q_hbm).start()
-
-    @pl.when(between)
-    def _():
-        a_copy(z, middle, 1, q_hbm).start()
+    a_copy(z, first, 0, q_hbm).start()
+    a_copy(z, second, 1, q_hbm).start()
 
     load_q.wait()
     load_g.wait()
@@ -179,46 +172,38 @@
     e_all[f] = lax.dot_general(
         pick, stored[...], (((0,), (0,)), ((), ())), preferred_element_type=jnp.float32
     ).astype(jnp.bfloat16)
-    e_copy(f, 0, across).start()
-    e_copy(f, 1, sibling).start()
+    push_e(0)
 
     @pl.when(jnp.logical_not(between))
     def _():
-        a_copy(z, near, 0, q_hbm).wait_send()
-        a_copy(z, middle, 1, q_hbm).start()
-
-    finish(0)
+        pass
+
     multiply(1)
     spread(1)
-    finish(1)
+    push_e(1)
+    finish(0)
     multiply(2)
     spread(2)
-    hand_on(0)
-    finish(2)
+    push_e(2)
+    finish(1)
     multiply(3)
     spread(3)
-    hand_on(1)
+    push_e(3)
+    finish(2)
     finish(3)
-    hand_on(2)
-    hand_on(3)
-    e_copy(across, 2, f).wait_recv()
-    e_copy(across, 2, sibling).start()
-    e_copy(sibling, 1, f).wait_recv()
-    e_copy((sibling + 2) % 4, 1, f).wait_recv()
+    for i in range(PARTS):
+        e_copy(across, 2, i, f).wait_recv()
+        e_copy(across, 2, i, sibling).start()
+    for i in range(PARTS):
+        e_copy(sibling, 1, i, f).wait_recv()
+        e_copy((sibling + 2) % 4, 1, i, f).wait_recv()
 
     total = None
     for s in range(n_blk):
         c = order[s]
-        if 0 < s < 3:
+        if s > 0:
             for j in range(n_blk):
                 c_copy(c, j, z, 0).wait_recv()
-        if s == 3:
-
-            @pl.when(jnp.logical_not(between))
-            def _():
-                for j in range(n_blk):
-                    c_copy(c, j, z, 0).wait_recv()
-
         rows = cond.shape[1] * cond.shape[2]
         value = contract(cond[c].reshape(rows, cond.shape[3]), e_all[c])
         total = value if total is None else total + value
@@ -230,23 +215,19 @@
     for j in range(n_blk):
         for d in range(1, n_feat):
             b_copy(j, f, (f + d) % n_feat).wait_send()
-        c_copy(z, j, near, 0).wait_send()
-        c_copy(z, j, middle, 1).wait_send()
+        for t in range(1, n_blk):
+            c_copy(z, j, order[t], t - 1).wait_send()
+    a_copy(z, first, 0).wait_send()
+    a_copy(z, second, 1).wait_send()
 
     @pl.when(between)
     def _():
-        for slot in range(4):
-            a_copy(z, near, slot).wait_send()
-        for j in range(n_blk):
-            c_copy(z, j, far, 2).wait_send()
-            c_copy(far, j, near, 3).wait_send()
-
-    @pl.when(jnp.logical_not(between))
-    def _():
-        a_copy(z, middle, 1).wait_send()
+        for slot in (2, 3):
+            a_copy(z, end, slot).wait_send()
 
     for slot in range(3):
-        e_copy(f, slot, sibling).wait_send()
+        for i in range(PARTS):
+            e_copy(f, slot, i, sibling).wait_send()
 
 
 def fused(n_blk, n_feat, queries, inv_gram, store, ids, mask):
@@ -274,8 +255,8 @@
             dma((5,)),
             dma((n_blk,)),
             dma((n_blk,)),
-            dma((3,)),
-            dma((n_feat,)),
+            dma((3, PARTS)),
+            dma((n_feat, PARTS)),
             dma((n_blk, n_feat)),
             dma((n_blk, n_feat)),
             dma((n_blk, n_blk)),

time: 46.3 us -> 32.7 us (0.71)
  Pallas kernels: 44.6 us -> 31 us
    pallas_call x1, Pallas kernels: 44.6 us -> 31 us  [fused(): pl.pallas_call(functools.partial(kernel, n_blk, n_feat), out_shape=jax.Sh...]
where the time goes in v3:
time: 32.7 us; the launch traced here: 32.5 us
  Pallas kernels  31 us (95%)
  other arithmetic  1.48 us (5%)
    pallas_call x1, Pallas kernels, fused(): pl.pallas_call(functools.partial(kernel, n_blk, n_feat), out_shape=jax.Sh...  31 us
    mul x1, other arithmetic, per_device(): return raw * example_weights[None, None, :]  1.48 us

profile of v3, /device:TPU:0, one launch (start us, length us, event | category | flops | bytes accessed | tf_op | source)
XLA Modules:
  0.0 32.5 jit_solution(1642626469729455541)
XLA Ops:
  0.0 0.0 copy-start
  0.0 31.0 %shard_map.64 = f32[4,16,256]{2,1,0:T(8,128)} custom-call(bf16[64,1024]{1,0:T(8,128)(2,1)} %q_hbm.1, bf16[1024,1024]{1,0:T(8,128)(2,1)} %g_hbm.1, bf16[512,1024]{1,0:T(8,128)(2,1)} %store_hbm.1, s32[1,256]{1,0:T(1,128)} %bitcast.2, s32[1,4]{1,0:T(1,128)} %bitcast.3), custom_call_target="tpu_custom_call" | custom-call | tf_op jit(solution)/shard_map/pallas_call | solution.py:240
  31.0 0.0 copy-done
  31.1 1.5 %broadcast_multiply_fusion = f32[4,16,256]{2,1,0:T(8,128)} fusion(f32[4,16,256]{2,1,0:T(8,128)} %shard_map.64, f32[256]{0:T(256)S(1)} %copy-done), kind=kLoop, calls=%fused_computation | loop fusion | flops 16384 | bytes 132096 | tf_op jit(solution)/shard_map/mul | solution.py:295
Async XLA Ops:
  0.0 31.0 %copy-start = (f32[256]{0:T(256)S(1)}, f32[256]{0:T(256)}, u32[]{:S(2)}) copy-start(f32[256]{0:T(256)} %param.10) | copy-start | bytes 3076

commit v4 on v3

--- a/solution.py
+++ b/solution.py
@@ -10,6 +10,7 @@
 MESH = pl.DeviceIdType.MESH
 VMEM = 63 * 1024 * 1024
 PARTS = 4
+HALVES = 2
 
 
 def contract(left, right):
@@ -87,14 +88,23 @@
     load_s.start()
     load_mask.start()
 
-    def a_copy(j, target, slot, src=None):
+    def a_copy(j, target, slot, i, src=None):
+        size = q_hbm.shape[0] // HALVES
+        rows = pl.ds(i * size, size)
         return send(
-            q_all.at[j] if src is None else src,
-            q_all.at[j],
-            a_send.at[slot],
-            a_recv.at[j],
+            q_all.at[j, rows] if src is None else src.at[rows],
+            q_all.at[j, rows],
+            a_send.at[slot, i],
+            a_recv.at[j, i],
             {"blk": target},
         )
+
+    def hand_on(s):
+        @pl.when(between)
+        def _():
+            for i in range(HALVES):
+                a_copy(order[s], z, 0, i).wait_recv()
+                a_copy(order[s], end, 2 + s // 2, i).start()
 
     def b_copy(j, src, target):
         return send(
@@ -126,14 +136,21 @@
             e_copy(f, 0, i, across).start()
             e_copy(f, 1, i, sibling).start()
 
+    def hand_over(i):
+        e_copy(across, 2, i, f).wait_recv()
+        e_copy(across, 2, i, sibling).start()
+
     def multiply(s):
         j = order[s]
-        if s > 0:
-            a_copy(j, z, 0).wait_recv()
-        if s % 2 == 1:
-            @pl.when(between)
+        if s == 2:
+            for i in range(HALVES):
+                a_copy(j, z, 0, i).wait_recv()
+        elif s > 0:
+
+            @pl.when(jnp.logical_not(between))
             def _():
-                a_copy(j, end, 2 + s // 2).start()
+                for i in range(HALVES):
+                    a_copy(j, z, 0, i).wait_recv()
 
         value = jnp.dot(q_all[j], gram[...], preferred_element_type=jnp.float32)
         rows = value.shape[0] // n_feat
@@ -155,8 +172,10 @@
             c_copy(z, j, order[t], t - 1).start()
 
     pl.semaphore_wait(barrier, n_blk + n_feat - 2)
-    a_copy(z, first, 0, q_hbm).start()
-    a_copy(z, second, 1, q_hbm).start()
+    for i in range(HALVES):
+        a_copy(z, first, 0, i, q_hbm).start()
+    for i in range(HALVES):
+        a_copy(z, second, 1, i, q_hbm).start()
 
     load_q.wait()
     load_g.wait()
@@ -173,11 +192,7 @@
         pick, stored[...], (((0,), (0,)), ((), ())), preferred_element_type=jnp.float32
     ).astype(jnp.bfloat16)
     push_e(0)
-
-    @pl.when(jnp.logical_not(between))
-    def _():
-        pass
-
+    hand_on(1)
     multiply(1)
     spread(1)
     push_e(1)
@@ -185,15 +200,17 @@
     multiply(2)
     spread(2)
     push_e(2)
+    hand_on(3)
     finish(1)
+    hand_over(0)
     multiply(3)
     spread(3)
     push_e(3)
+    hand_over(1)
     finish(2)
+    hand_over(2)
     finish(3)
-    for i in range(PARTS):
-        e_copy(across, 2, i, f).wait_recv()
-        e_copy(across, 2, i, sibling).start()
+    hand_over(3)
     for i in range(PARTS):
         e_copy(sibling, 1, i, f).wait_recv()
         e_copy((sibling + 2) % 4, 1, i, f).wait_recv()
@@ -217,13 +234,15 @@
             b_copy(j, f, (f + d) % n_feat).wait_send()
         for t in range(1, n_blk):
             c_copy(z, j, order[t], t - 1).wait_send()
-    a_copy(z, first, 0).wait_send()
-    a_copy(z, second, 1).wait_send()
+    for i in range(HALVES):
+        a_copy(z, first, 0, i).wait_send()
+        a_copy(z, second, 1, i).wait_send()
 
     @pl.when(between)
     def _():
-        for slot in (2, 3):
-            a_copy(z, end, slot).wait_send()
+        for i in range(HALVES):
+            a_copy(z, end, 2, i).wait_send()
+            a_copy(z, end, 3, i).wait_send()
 
     for slot in range(3):
         for i in range(PARTS):
@@ -253,8 +272,8 @@
             pltpu.VMEM((n_blk, n_feat, rows, inv_gram.shape[1]), jnp.bfloat16),
             pltpu.VMEM((n_blk, n_blk, rows, inv_gram.shape[1]), jnp.bfloat16),
             dma((5,)),
-            dma((n_blk,)),
-            dma((n_blk,)),
+            dma((4, HALVES)),
+            dma((n_blk, HALVES)),
             dma((3, PARTS)),
             dma((n_feat, PARTS)),
             dma((n_blk, n_feat)),

time: 32.7 us -> 30.6 us (0.936)
  Pallas kernels: 31 us -> 29 us
    pallas_call x1, Pallas kernels: 31 us -> 29 us  [fused(): pl.pallas_call(functools.partial(kernel, n_blk, n_feat), out_shape=jax.Sh...]
where the time goes in v4:
time: 30.6 us; the launch traced here: 30.5 us
  Pallas kernels  29 us (95%)
  other arithmetic  1.48 us (5%)
    pallas_call x1, Pallas kernels, fused(): pl.pallas_call(functools.partial(kernel, n_blk, n_feat), out_shape=jax.Sh...  29 us
    mul x1, other arithmetic, per_device(): return raw * example_weights[None, None, :]  1.48 us

profile of v4, /device:TPU:0, one launch (start us, length us, event | category | flops | bytes accessed | tf_op | source)
XLA Modules:
  0.0 30.5 jit_solution(17953962056833595617)
XLA Ops:
  0.0 0.0 copy-start
  0.0 29.0 %shard_map.64 = f32[4,16,256]{2,1,0:T(8,128)} custom-call(bf16[64,1024]{1,0:T(8,128)(2,1)} %q_hbm.1, bf16[1024,1024]{1,0:T(8,128)(2,1)} %g_hbm.1, bf16[512,1024]{1,0:T(8,128)(2,1)} %store_hbm.1, s32[1,256]{1,0:T(1,128)} %bitcast.2, s32[1,4]{1,0:T(1,128)} %bitcast.3), custom_call_target="tpu_custom_call" | custom-call | tf_op jit(solution)/shard_map/pallas_call | solution.py:259
  29.0 0.0 copy-done
  29.0 1.5 %broadcast_multiply_fusion = f32[4,16,256]{2,1,0:T(8,128)} fusion(f32[4,16,256]{2,1,0:T(8,128)} %shard_map.64, f32[256]{0:T(256)S(1)} %copy-done), kind=kLoop, calls=%fused_computation | loop fusion | flops 16384 | bytes 132096 | tf_op jit(solution)/shard_map/mul | solution.py:314
Async XLA Ops:
  0.0 29.0 %copy-start = (f32[256]{0:T(256)S(1)}, f32[256]{0:T(256)}, u32[]{:S(2)}) copy-start(f32[256]{0:T(256)} %param.10) | copy-start | bytes 3076

commit v5 on v4

--- a/solution.py
+++ b/solution.py
@@ -211,16 +211,17 @@
     hand_over(2)
     finish(3)
     hand_over(3)
-    for i in range(PARTS):
-        e_copy(sibling, 1, i, f).wait_recv()
-        e_copy((sibling + 2) % 4, 1, i, f).wait_recv()
-
     total = None
-    for s in range(n_blk):
-        c = order[s]
-        if s > 0:
+    for s, c in enumerate((f, sibling, across, (sibling + 2) % 4)):
+        if s % 2 == 1:
+            for i in range(PARTS):
+                e_copy(c, 1, i, f).wait_recv()
+
+        @pl.when(c != z)
+        def _():
             for j in range(n_blk):
                 c_copy(c, j, z, 0).wait_recv()
+
         rows = cond.shape[1] * cond.shape[2]
         value = contract(cond[c].reshape(rows, cond.shape[3]), e_all[c])
         total = value if total is None else total + value

time: 30.6 us -> 30.6 us (level)
  no operation moved by 1% of the time
where the time goes in v5:
time: 30.6 us; the launch traced here: 30.5 us
  Pallas kernels  29 us (95%)
  other arithmetic  1.48 us (5%)
    pallas_call x1, Pallas kernels, fused(): pl.pallas_call(functools.partial(kernel, n_blk, n_feat), out_shape=jax.Sh...  29 us
    mul x1, other arithmetic, per_device(): return raw * example_weights[None, None, :]  1.48 us

profile of v5, /device:TPU:0, one launch (start us, length us, event | category | flops | bytes accessed | tf_op | source)
XLA Modules:
  0.0 30.5 jit_solution(1004416869499170379)
XLA Ops:
  0.0 0.0 copy-start
  0.0 29.0 %shard_map.64 = f32[4,16,256]{2,1,0:T(8,128)} custom-call(bf16[64,1024]{1,0:T(8,128)(2,1)} %q_hbm.1, bf16[1024,1024]{1,0:T(8,128)(2,1)} %g_hbm.1, bf16[512,1024]{1,0:T(8,128)(2,1)} %store_hbm.1, s32[1,256]{1,0:T(1,128)} %bitcast.2, s32[1,4]{1,0:T(1,128)} %bitcast.3), custom_call_target="tpu_custom_call" | custom-call | tf_op jit(solution)/shard_map/pallas_call | solution.py:260
  29.0 0.0 copy-done
  29.0 1.5 %broadcast_multiply_fusion = f32[4,16,256]{2,1,0:T(8,128)} fusion(f32[4,16,256]{2,1,0:T(8,128)} %shard_map.64, f32[256]{0:T(256)S(1)} %copy-done), kind=kLoop, calls=%fused_computation | loop fusion | flops 16384 | bytes 132096 | tf_op jit(solution)/shard_map/mul | solution.py:315
Async XLA Ops:
  0.0 29.0 %copy-start = (f32[256]{0:T(256)S(1)}, f32[256]{0:T(256)}, u32[]{:S(2)}) copy-start(f32[256]{0:T(256)} %param.10) | copy-start | bytes 3076
